TPU v7x, 32 devices: a whole 2x2x4 slice. The times are simulated.
32 devices in a mesh: freq: 8 (over z, x), bl: 4 (over y, core).
Axes of the slice: x: 2, y: 2, z: 4, core: 2. Of those that a mesh axis runs over, the one named last changes fastest.
Arguments:
- voltages: bfloat16 [1024, 134144], P(('bl', 'freq')), may hold values from -6 to 6
- fir_taps: float32 [4, 1024], replicated, may hold values from -3 to 3
- antenna_order: int32 [1024], replicated, may hold values from 0 to 1023, each once
- tile_list: int32 [4, 2], replicated, may hold values from 0 to 3
Outputs:
- visibilities: bfloat16 [4, 512, 256, 512], P('bl', 'freq')
All inputs are finite; a program needn't handle non-finite values.
Results may differ from a plain program's by a relative error of at most 0.0074.
Values may be sent and summed in bfloat16 or wider, within the bound.
A program may use at most 128 MiB of HBM per device.

v0:
```python
import math
import jax
import jax.numpy as jnp
from jax import lax
from jax.sharding import PartitionSpec as P

K = 1024
TAPS = 4
PANEL = 256
SAMPLES = 128


def make_table(points, kept):
    product = (
        jnp.arange(points, dtype=jnp.int32)[:, None]
        * jnp.arange(kept, dtype=jnp.int32)[None, :]
        % points
    )
    phase = 2.0 * math.pi / points * product.astype(jnp.float32)
    return jnp.concatenate([jnp.cos(phase), -jnp.sin(phase)], axis=1).astype(jnp.bfloat16)


def arrange(panel):
    width = panel.shape[1]
    return jnp.transpose(panel, (3, 0, 2, 1)).reshape(panel.shape[3], panel.shape[0], 2 * width)


def rotated(panel):
    turned = jnp.stack([-panel[:, :, 1, :], panel[:, :, 0, :]], axis=2)
    return arrange(turned)


def correlate(source, antenna_order, tile):
    row_ids = lax.dynamic_slice_in_dim(antenna_order, tile[0] * PANEL, PANEL)
    col_ids = lax.dynamic_slice_in_dim(antenna_order, tile[1] * PANEL, PANEL)
    row_panel = jnp.take(source, row_ids, axis=0)
    col_panel = jnp.take(source, col_ids, axis=0)
    left = arrange(row_panel)
    right = jnp.concatenate([arrange(col_panel), rotated(col_panel)], axis=1)
    return jnp.einsum("fps,fqs->fpq", left, right, preferred_element_type=jnp.float32)


def per_device(voltages, fir_taps, antenna_order, tile_list):
    local_count = voltages.shape[0]
    frames = voltages.reshape(local_count, SAMPLES + TAPS - 1, K)
    filtered = jnp.zeros((local_count, SAMPLES, K), jnp.float32)
    for tap in range(TAPS):
        filtered = filtered + fir_taps[tap][None, None, :] * frames[
            :, tap : tap + SAMPLES, :
        ].astype(jnp.float32)
    filtered = filtered.astype(jnp.bfloat16)
    table = make_table(K, K // 2)
    spectra = jnp.dot(
        filtered.reshape(local_count * SAMPLES, K), table, preferred_element_type=jnp.float32
    )
    spectra = (
        (spectra * (1.0 / math.sqrt(K)))
        .astype(jnp.bfloat16)
        .reshape(local_count, SAMPLES, 2, K // 2)
    )
    turned = lax.all_to_all(spectra, "freq", split_axis=3, concat_axis=0, tiled=True)
    gathered = lax.all_gather(turned, "bl", axis=0, tiled=True)
    own_tile = tile_list[lax.axis_index("bl")]
    summed = correlate(gathered, antenna_order, own_tile)
    return (summed / SAMPLES).astype(jnp.bfloat16)[None]


def solution(mesh):
    return jax.shard_map(
        per_device,
        mesh=mesh,
        in_specs=(P(("bl", "freq"), None), P(), P(), P()),
        out_specs=P("bl", "freq", None, None),
        check_vma=False,
    )
```

profile of v0, /device:TPU:0, one launch (start us, length us, event | category | flops | bytes accessed | tf_op | source)
XLA Modules:
  0.0 656.6 jit_solution(10840728497448380260)
XLA Ops:
  6.5 8.5 %negate_convert_fusion = (bf16[1024,512]{1,0:T(8,128)(2,1)S(1)}, bf16[1024,512]{1,0:T(8,128)(2,1)S(1)}) fusion(), kind=kLoop, calls=%fused_computation.23 | loop fusion | flops 8912896 | bytes 2097152 | tf_op jit(solution)/shard_map/convert.1
  15.1 9.2 %reshape.35 = bf16[32,131,1024]{2,1,0:T(8,128)(2,1)} reshape(bf16[32,134144]{1,0:T(8,128)(2,1)} %param.6) | data formatting | bytes 17170432 | tf_op jit(solution)/shard_map/reshape | solution.py:45
  24.3 19.3 %add_convert_fusion = bf16[32,128,1024]{2,1,0:T(8,128)(2,1)S(1)} fusion(bf16[32,131,1024]{2,1,0:T(8,128)(2,1)} %reshape.35, f32[1024]{0:T(1024)S(1)} %bitcast.28, f32[1024]{0:T(1024)S(1)} %bitcast.29, f32[1024]{0:T(1024)S(1)} %bitcast.27, f32[1024]{0:T(1024)S(1)} %bitcast.26), kind=kLoop, calls=%fused_computation.9 | loop fusion | flops 50331648 | bytes 41959424 | tf_op jit(solution)/shard_map/convert_element_type | solution.py:51
  43.6 11.0 %multiply_convert_fusion.1 = bf16[4096,1024]{1,0:T(8,128)(2,1)} fusion(bf16[4096,1024]{1,0:T(8,128)(2,1)S(1)} %bitcast.24, bf16[1024,512]{1,0:T(8,128)(2,1)S(1)} %get-tuple-element.20, bf16[1024,512]{1,0:T(8,128)(2,1)S(1)} %get-tuple-element.21), kind=kOutput, calls=%fused_computation.8 | convolution fusion | flops 8602517504 | bytes 18874368 | tf_op jit(solution)/shard_map/dot_general | solution.py:53
  54.6 14.5 %reshape.37 = bf16[32,128,2,512]{3,2,1,0:T(2,128)(2,1)} reshape(bf16[4096,1024]{1,0:T(8,128)(2,1)} %multiply_convert_fusion.1) | data formatting | bytes 16777216 | tf_op jit(solution)/shard_map/reshape | solution.py:59
  69.1 28.1 %copy.15 = bf16[32,128,2,512]{1,2,0,3:T(2,128)(2,1)} copy(bf16[32,128,2,512]{3,2,1,0:T(2,128)(2,1)} %reshape.37) | data formatting | bytes 16777216 | tf_op jit(solution)/shard_map/reshape | solution.py:59
  97.2 190.4 %all_to_all.18 = bf16[32,128,2,512]{1,2,0,3:T(2,128)(2,1)} all-to-all(bf16[32,128,2,512]{1,2,0,3:T(2,128)(2,1)} %copy.15), channel_id=1, replica_groups=mesh['freq'=8,'bl'=4] {'freq'}, dimensions={3} | all-to-all | bytes 16777216 | tf_op jit(solution)/shard_map/all_to_all | solution.py:61
  287.6 16.5 %copy.16 = bf16[32,128,2,512]{1,3,2,0:T(8,128)(2,1)} copy(bf16[32,128,2,512]{1,2,0,3:T(2,128)(2,1)} %all_to_all.18) | data formatting | bytes 16777216 | tf_op jit(solution)/shard_map/all_to_all | solution.py:61
  304.1 9.8 %copy.17 = bf16[8,32,128,2,64]{2,4,3,1,0:T(8,128)(2,1)} copy(bf16[8,32,128,2,64]{2,4,0,3,1:T(8,128)(2,1)} %bitcast.23) | data formatting | bytes 16777216 | tf_op jit(solution)/shard_map/all_to_all | solution.py:61
  314.0 0.5 fusion.19
  315.9 198.8 %all-gather.2.cloned.1.call-done = bf16[1024,128,2,64]{1,3,2,0:T(8,128)(2,1)} async-done(((bf16[256,128,2,64]{1,3,2,0:T(8,128)(2,1)}), bf16[1024,128,2,64]{1,3,2,0:T(8,128)(2,1)}) %all-gather.2.cloned.1.call-update) | async-done | bytes 33554448 | tf_op jit(solution)/shard_map/all_gather | solution.py:62
  514.7 9.1 %gather_fusion.1 = bf16[256,128,2,64]{1,3,2,0:T(8,128)(2,1)} fusion(bf16[1024,128,2,64]{1,3,2,0:T(8,128)(2,1)} %all-gather.2.cloned.1.call-done, s32[1024]{0:T(1024)S(1)} %get-tuple-element.22), kind=kCustom, calls=%fused_computation.1.clone | custom fusion | bytes 16778240 | tf_op jit(solution)/shard_map/jit(_take)/gather | solution.py:37
  523.8 7.4 %broadcast_select_fusion = bf16[256,128,2,64]{1,3,2,0:T(8,128)(2,1)} fusion(bf16[256,128,2,64]{1,3,2,0:T(8,128)(2,1)} %gather_fusion.1, pred[256]{0:T(512)(128)(4,1)S(1)} %get-tuple-element.6), kind=kLoop, calls=%fused_computation.12 | loop fusion | flops 4194304 | bytes 16777472 | tf_op jit(solution)/shard_map/jit(_take)/select_n | solution.py:37
  531.3 7.4 %fusion.22 = bf16[64,256,2,128]{3,0,2,1:T(8,128)(2,1)} fusion(bf16[256,128,2,64]{1,3,2,0:T(8,128)(2,1)} %gather_fusion.1, pred[256]{0:T(512)(128)(4,1)S(1)} %get-tuple-element.6), kind=kLoop, calls=%fused_computation.39 | loop fusion | flops 4194304 | bytes 16777472 | tf_op jit(solution)/shard_map/transpose | solution.py:25
  538.7 9.1 %gather_fusion = bf16[256,128,2,64]{1,3,2,0:T(8,128)(2,1)} fusion(bf16[1024,128,2,64]{1,3,2,0:T(8,128)(2,1)} %all-gather.2.cloned.1.call-done, s32[1024]{0:T(1024)S(1)} %get-tuple-element.23), kind=kCustom, calls=%fused_computation.clone | custom fusion | bytes 16778240 | tf_op jit(solution)/shard_map/jit(_take)/gather | solution.py:36
  547.8 7.6 %select_bitcast_fusion = bf16[64,256,2,128]{3,0,2,1:T(8,128)(2,1)} fusion(bf16[256,128,2,64]{1,3,2,0:T(8,128)(2,1)} %gather_fusion, pred[256]{0:T(512)(128)(4,1)S(1)} %get-tuple-element.16), kind=kLoop, calls=%fused_computation.11 | loop fusion | flops 4194304 | bytes 16777472 | tf_op jit(solution)/shard_map/transpose | solution.py:25
  555.4 12.9 %copy.18 = bf16[64,256,2,128]{1,3,2,0:T(8,128)(2,1)} copy(bf16[64,256,2,128]{3,0,2,1:T(8,128)(2,1)} %select_bitcast_fusion) | data formatting | bytes 16777216 | tf_op jit(solution)/shard_map/transpose | solution.py:25
  568.3 5.2 slice_negate_fusion
  573.6 6.5 maximum_bitcast_fusion
  580.0 13.2 %copy.20 = bf16[64,256,2,128]{3,2,1,0:T(2,128)(2,1)} copy(bf16[64,256,2,128]{3,0,2,1:T(8,128)(2,1)} %maximum_bitcast_fusion) | data formatting | bytes 16777216 | tf_op jit(solution)/shard_map/transpose | solution.py:25
  593.2 14.1 %reshape.40 = bf16[64,256,256]{2,1,0:T(8,128)(2,1)} reshape(bf16[64,256,2,128]{3,2,1,0:T(2,128)(2,1)} %copy.20) | data formatting | bytes 16777216 | tf_op jit(solution)/shard_map/reshape | solution.py:25
  607.3 13.2 %copy.19 = bf16[64,256,2,128]{3,2,1,0:T(2,128)(2,1)} copy(bf16[64,256,2,128]{3,0,2,1:T(8,128)(2,1)} %fusion.22) | data formatting | bytes 16777216 | tf_op jit(solution)/shard_map/transpose | solution.py:25
  620.4 14.1 %reshape.39 = bf16[64,256,256]{2,1,0:T(8,128)(2,1)} reshape(bf16[64,256,2,128]{3,2,1,0:T(2,128)(2,1)} %copy.19) | data formatting | bytes 16777216 | tf_op jit(solution)/shard_map/reshape | solution.py:25
  634.5 15.2 %fusion = bf16[1,64,256,512]{3,2,1,0:T(8,128)(2,1)} fusion(bf16[64,256,256]{1,2,0:T(8,128)(2,1)} %bitcast.25, bf16[64,256,256]{2,1,0:T(8,128)(2,1)} %reshape.40, bf16[64,256,256]{2,1,0:T(8,128)(2,1)} %reshape.39), kind=kOutput, calls=%fused_computation.3 | convolution fusion | flops 4345298944 | bytes 41943040 | tf_op jit(solution)/shard_map/fps,fqs->fpq/dot_general | solution.py:40
  (14 shorter events, 0.2 us)
Async XLA Ops:
  6.5 307.4 %copy-start = (s32[4,2]{0,1:T(2,128)S(1)}, s32[4,2]{0,1:T(2,128)}, u32[]{:S(2)}) copy-start(s32[4,2]{0,1:T(2,128)} %param.9) | copy-start | bytes 100
  6.5 508.2 %all-gather.2.cloned.1.call-start = ((), (), s32[]{:S(2)}) async-start(), calls=%async_computation.1 | async-start | bytes 41943040 | tf_op jit(solution)/shard_map/all_gather | solution.py:62
  15.1 9.2 %copy-start.2 = (f32[4,1024]{1,0:T(4,128)S(1)}, f32[4,1024]{1,0:T(4,128)}, u32[]{:S(2)}) copy-start(f32[4,1024]{1,0:T(4,128)} %param.7) | copy-start | bytes 49156
  313.9 1.9 copy-start.3
  634.5 15.2 %copy-start.1 = (s32[4,2]{0,1:T(2,128)S(1)}, s32[4,2]{0,1:T(2,128)}, u32[]{:S(2)}) copy-start(s32[4,2]{0,1:T(2,128)} %param.9) | copy-start | bytes 100
Sparse Core Ops, SparseCore 0:
  314.0 200.6 all-gather.1
where the time goes:
time: 659 us; the launch traced here: 657 us
  waiting for transfers between devices  199 us (30%)
  blocking collectives  190 us (29%)
  local copies, waits for them, and re-layouts  164 us (25%)
  other arithmetic  62.1 us (9%)
  matrix products  26.2 us (4%)
  between operations  14.7 us (2%)
    all_gather x1, waiting for transfers between devices, per_device(): gathered = lax.all_gather(turned, 'bl', axis=0, tiled=True)  199 us
    all_to_all x1, blocking collectives, per_device(): lax.all_to_all(spectra, 'freq', split_axis=3, concat_axis=0, tiled=True)  190 us
    reshape x2, local copies, waits for them, and re-layouts, per_device(): spectra = (spectra * (1.0 / math.sqrt(K))).astype(jnp.bfloat16).reshape(l...  42.6 us
    transpose x3, local copies, waits for them, and re-layouts, arrange(): jnp.transpose(panel, (3, 0, 2, 1))  39.3 us
    reshape x2, local copies, waits for them, and re-layouts, arrange(): jnp.transpose(panel, (3, 0, 2, 1))  28.2 us
    all_to_all x2, local copies, waits for them, and re-layouts, per_device(): lax.all_to_all(spectra, 'freq', split_axis=3, concat_axis=0, tiled=True)  26.3 us
    transpose x3, other arithmetic, arrange(): jnp.transpose(panel, (3, 0, 2, 1))  21.5 us
    convert_element_type x1, other arithmetic, per_device(): filtered = filtered.astype(jnp.bfloat16)  19.3 us
  transfers between devices with their start and end apart: 1, of which 1 were waited for; matrix products, arithmetic and copies ran while one was open for 0% of the time, Pallas kernels for 0%

commit v1 on v0

--- a/solution.py
+++ b/solution.py
@@ -1,3 +1,4 @@
+import functools
 import math
 import jax
 import jax.numpy as jnp
@@ -8,6 +9,38 @@
 TAPS = 4
 PANEL = 256
 SAMPLES = 128
+
+
+def _load_plate(x_local, dev_axis):
+    met_up = lax.axis_index(dev_axis)
+    fresh = lax.axis_size(dev_axis)
+    cards = []
+    current_value, mixed_arr, tile_out = (fresh, met_up, x_local.shape[0])
+    for nth, dd in enumerate(x_local.shape):
+        cards.append(dd * current_value if nth == 0 else dd)
+    r1 = jnp.zeros(cards, x_local.dtype)
+    field_out = f_now = x_local
+    x_new = lax.dynamic_update_slice_in_dim(r1, x_local, mixed_arr * tile_out, axis=0)
+    for it in range(1, current_value // 2 + 1):
+        leaves = []
+        for nth in range(current_value):
+            leaves.append((nth, (nth + 1) % current_value))
+        field_out = lax.ppermute(field_out, dev_axis, perm=leaves)
+        x_new = lax.dynamic_update_slice_in_dim(
+            x_new, field_out, (mixed_arr - it) % current_value * tile_out, axis=0
+        )
+        if 2 * it < current_value:
+            line_up = []
+            for nth in range(current_value):
+                line_up.append((nth, (nth - 1) % current_value))
+            f_now = lax.ppermute(f_now, axis_name=dev_axis, perm=line_up)
+            x_new = lax.dynamic_update_slice_in_dim(
+                x_new, f_now, (mixed_arr + it) % current_value * tile_out, axis=0
+            )
+    return x_new
+
+
+replace_strings = functools.partial(_load_plate, dev_axis="bl")
 
 
 def make_table(points, kept):
@@ -59,7 +92,7 @@
         .reshape(local_count, SAMPLES, 2, K // 2)
     )
     turned = lax.all_to_all(spectra, "freq", split_axis=3, concat_axis=0, tiled=True)
-    gathered = lax.all_gather(turned, "bl", axis=0, tiled=True)
+    gathered = replace_strings(turned)
     own_tile = tile_list[lax.axis_index("bl")]
     summed = correlate(gathered, antenna_order, own_tile)
     return (summed / SAMPLES).astype(jnp.bfloat16)[None]

time: 659 us -> 738 us (1.12)
  local copies, waits for them, and re-layouts: 164 us -> 219 us
  waiting for transfers between devices: 199 us -> 227 us
  between operations: 14.7 us -> 1.59 us
    ppermute x0 -> x3, waiting for transfers between devices: none -> 227 us  [the longest x2 227 us: _load_plate(): field_out = lax.ppermute(field_out, dev_axis, perm=leaves)]
    all_gather x1 -> x0, waiting for transfers between devices: 199 us -> none  [per_device(): gathered = lax.all_gather(turned, 'bl', axis=0, tiled=True)]
    dynamic_update_slice x0 -> x4, local copies, waits for them, and re-layouts: none -> 42.4 us  [the longest x2 21.2 us: _load_plate(): lax.dynamic_update_slice_in_dim(x_new, field_out, (mixed_arr - it) % curr...]
    broadcast_in_dim x0 -> x1, local copies, waits for them, and re-layouts: none -> 11.3 us  [_load_plate(): r1 = jnp.zeros(cards, x_local.dtype)]
  transfers between devices with their start and end apart: 1 -> 3, of which waited for: 1 -> 2; matrix products, arithmetic and copies ran while one was open for 0% -> 6% of each run, Pallas kernels for 0% -> 0%
where the time goes in v1:
time: 738 us; the launch traced here: 729 us
  waiting for transfers between devices  227 us (31%)
  local copies, waits for them, and re-layouts  219 us (30%)
  blocking collectives  190 us (26%)
  other arithmetic  62.1 us (8%)
  matrix products  26.2 us (4%)
    ppermute x2, waiting for transfers between devices, _load_plate(): field_out = lax.ppermute(field_out, dev_axis, perm=leaves)  227 us
    all_to_all x1, blocking collectives, per_device(): lax.all_to_all(spectra, 'freq', split_axis=3, concat_axis=0, tiled=True)  190 us
    reshape x2, local copies, waits for them, and re-layouts, per_device(): spectra = (spectra * (1.0 / math.sqrt(K))).astype(jnp.bfloat16).reshape(l...  42.6 us
    transpose x3, local copies, waits for them, and re-layouts, arrange(): jnp.transpose(panel, (3, 0, 2, 1))  39.2 us
    reshape x2, local copies, waits for them, and re-layouts, arrange(): jnp.transpose(panel, (3, 0, 2, 1))  28.1 us
    all_to_all x2, local copies, waits for them, and re-layouts, per_device(): lax.all_to_all(spectra, 'freq', split_axis=3, concat_axis=0, tiled=True)  26.3 us
    transpose x3, other arithmetic, arrange(): jnp.transpose(panel, (3, 0, 2, 1))  21.5 us
    dynamic_update_slice x2, local copies, waits for them, and re-layouts, _load_plate(): lax.dynamic_update_slice_in_dim(x_new, field_out, (mixed_arr - it) % curr...  21.2 us
  transfers between devices with their start and end apart: 3, of which 2 were waited for; matrix products, arithmetic and copies ran while one was open for 6% of the time, Pallas kernels for 0%

profile of v1, /device:TPU:0, one launch (start us, length us, event | category | flops | bytes accessed | tf_op | source)
XLA Modules:
  0.0 728.5 jit_solution(18148771104185487079)
XLA Ops:
  0.0 8.5 %negate_convert_fusion = (bf16[1024,512]{1,0:T(8,128)(2,1)S(1)}, bf16[1024,512]{1,0:T(8,128)(2,1)S(1)}) fusion(), kind=kLoop, calls=%fused_computation.23 | loop fusion | flops 8912896 | bytes 2097152 | tf_op jit(solution)/shard_map/convert.1
  9.4 9.2 %reshape.35 = bf16[32,131,1024]{2,1,0:T(8,128)(2,1)} reshape(bf16[32,134144]{1,0:T(8,128)(2,1)} %param.6) | data formatting | bytes 17170432 | tf_op jit(solution)/shard_map/reshape | solution.py:78
  18.7 19.3 %add_convert_fusion = bf16[32,128,1024]{2,1,0:T(8,128)(2,1)S(1)} fusion(bf16[32,131,1024]{2,1,0:T(8,128)(2,1)} %reshape.35, f32[1024]{0:T(1024)S(1)} %bitcast.30, f32[1024]{0:T(1024)S(1)} %bitcast.31, f32[1024]{0:T(1024)S(1)} %bitcast.29, f32[1024]{0:T(1024)S(1)} %bitcast.28), kind=kLoop, calls=%fused_computation.9 | loop fusion | flops 50331648 | bytes 41959424 | tf_op jit(solution)/shard_map/convert_element_type | solution.py:84
  38.0 11.0 %multiply_convert_fusion.1 = bf16[4096,1024]{1,0:T(8,128)(2,1)} fusion(bf16[4096,1024]{1,0:T(8,128)(2,1)S(1)} %bitcast.26, bf16[1024,512]{1,0:T(8,128)(2,1)S(1)} %get-tuple-element.20, bf16[1024,512]{1,0:T(8,128)(2,1)S(1)} %get-tuple-element.21), kind=kOutput, calls=%fused_computation.8 | convolution fusion | flops 8602517504 | bytes 18874368 | tf_op jit(solution)/shard_map/dot_general | solution.py:86
  48.9 14.5 %reshape.37 = bf16[32,128,2,512]{3,2,1,0:T(2,128)(2,1)} reshape(bf16[4096,1024]{1,0:T(8,128)(2,1)} %multiply_convert_fusion.1) | data formatting | bytes 16777216 | tf_op jit(solution)/shard_map/reshape | solution.py:92
  63.4 28.1 %copy.15 = bf16[32,128,2,512]{1,2,0,3:T(2,128)(2,1)} copy(bf16[32,128,2,512]{3,2,1,0:T(2,128)(2,1)} %reshape.37) | data formatting | bytes 16777216 | tf_op jit(solution)/shard_map/reshape | solution.py:92
  91.5 190.4 %all_to_all.18 = bf16[32,128,2,512]{1,2,0,3:T(2,128)(2,1)} all-to-all(bf16[32,128,2,512]{1,2,0,3:T(2,128)(2,1)} %copy.15), channel_id=1, replica_groups=mesh['freq'=8,'bl'=4] {'freq'}, dimensions={3} | all-to-all | bytes 16777216 | tf_op jit(solution)/shard_map/all_to_all | solution.py:94
  281.9 16.5 %copy.16 = bf16[32,128,2,512]{1,3,2,0:T(8,128)(2,1)} copy(bf16[32,128,2,512]{1,2,0,3:T(2,128)(2,1)} %all_to_all.18) | data formatting | bytes 16777216 | tf_op jit(solution)/shard_map/all_to_all | solution.py:94
  298.4 9.8 %copy.17 = bf16[8,32,128,2,64]{2,4,3,1,0:T(8,128)(2,1)} copy(bf16[8,32,128,2,64]{2,4,0,3,1:T(8,128)(2,1)} %bitcast.25) | data formatting | bytes 16777216 | tf_op jit(solution)/shard_map/all_to_all | solution.py:94
  309.9 179.4 %collective-permute-done = bf16[256,128,2,64]{1,3,2,0:T(8,128)(2,1)} collective-permute-done((bf16[256,128,2,64]{1,3,2,0:T(8,128)(2,1)}, bf16[256,128,2,64]{1,3,2,0:T(8,128)(2,1)}, u32[]{:S(2)}, u32[]{:S(2)}) %collective-permute-start) | collective-permute-done | bytes 8388640 | tf_op jit(solution)/shard_map/ppermute | solution.py:28
  491.8 11.3 %broadcast_in_dim.17 = bf16[1024,128,2,64]{1,3,2,0:T(8,128)(2,1)} broadcast(bf16[]{:T(256)} %constant.56.clone.1), dimensions={} | broadcast | bytes 33554432 | tf_op jit(solution)/shard_map/broadcast_in_dim | solution.py:21
  503.0 10.6 %constant_dynamic-update-slice_fusion.3 = bf16[1024,128,2,64]{1,3,2,0:T(8,128)(2,1)} fusion(bf16[1024,128,2,64]{1,3,2,0:T(8,128)(2,1)} %broadcast_in_dim.17, bf16[256,128,2,64]{1,3,2,0:T(8,128)(2,1)} %bitcast.24, s32[]{:T(128)S(6)} %select_n.52), kind=kLoop, calls=%fused_computation.38 | loop fusion | bytes 16777220 | tf_op jit(solution)/shard_map/dynamic_update_slice | solution.py:23
  513.6 10.6 %constant_dynamic-update-slice_fusion.2 = bf16[1024,128,2,64]{1,3,2,0:T(8,128)(2,1)} fusion(bf16[1024,128,2,64]{1,3,2,0:T(8,128)(2,1)} %constant_dynamic-update-slice_fusion.3, bf16[256,128,2,64]{1,3,2,0:T(8,128)(2,1)} %collective-permute-done, s32[]{:T(128)S(6)} %select_n.54), kind=kLoop, calls=%fused_computation.37 | loop fusion | bytes 16777220 | tf_op jit(solution)/shard_map/dynamic_update_slice | solution.py:29
  524.2 10.6 %constant_dynamic-update-slice_fusion.1 = bf16[1024,128,2,64]{1,3,2,0:T(8,128)(2,1)} fusion(bf16[1024,128,2,64]{1,3,2,0:T(8,128)(2,1)} %constant_dynamic-update-slice_fusion.2, bf16[256,128,2,64]{1,3,2,0:T(8,128)(2,1)} %collective-permute-done.1, s32[]{:T(128)S(6)} %select_n.56), kind=kLoop, calls=%fused_computation.36 | loop fusion | bytes 16777220 | tf_op jit(solution)/shard_map/dynamic_update_slice | solution.py:37
  534.9 47.7 %collective-permute-done.2 = bf16[256,128,2,64]{1,3,2,0:T(8,128)(2,1)} collective-permute-done((bf16[256,128,2,64]{1,3,2,0:T(8,128)(2,1)}, bf16[256,128,2,64]{1,3,2,0:T(8,128)(2,1)}, u32[]{:S(2)}, u32[]{:S(2)}) %collective-permute-start.2) | collective-permute-done | bytes 8388640 | tf_op jit(solution)/shard_map/ppermute | solution.py:28
  582.5 10.6 %constant_dynamic-update-slice_fusion = bf16[1024,128,2,64]{1,3,2,0:T(8,128)(2,1)} fusion(bf16[1024,128,2,64]{1,3,2,0:T(8,128)(2,1)} %constant_dynamic-update-slice_fusion.1, bf16[256,128,2,64]{1,3,2,0:T(8,128)(2,1)} %collective-permute-done.2, s32[]{:T(128)S(6)} %select_n.58), kind=kLoop, calls=%fused_computation.35 | loop fusion | bytes 16777220 | tf_op jit(solution)/shard_map/dynamic_update_slice | solution.py:29
  593.1 9.3 %gather_fusion.1 = bf16[256,128,2,64]{1,3,2,0:T(8,128)(2,1)} fusion(bf16[1024,128,2,64]{1,3,2,0:T(8,128)(2,1)} %constant_dynamic-update-slice_fusion, s32[1024]{0:T(1024)S(1)} %get-tuple-element.22), kind=kCustom, calls=%fused_computation.1.clone | custom fusion | bytes 16778240 | tf_op jit(solution)/shard_map/jit(_take)/gather | solution.py:70
  629.0 13.2 %copy.20 = bf16[64,256,2,128]{3,2,1,0:T(2,128)(2,1)} copy(bf16[64,256,2,128]{3,0,2,1:T(8,128)(2,1)} %maximum_bitcast_fusion) | data formatting | bytes 16777216 | tf_op jit(solution)/shard_map/transpose | solution.py:58
  642.2 14.0 %reshape.40 = bf16[64,256,256]{2,1,0:T(8,128)(2,1)} reshape(bf16[64,256,2,128]{3,2,1,0:T(2,128)(2,1)} %copy.20) | data formatting | bytes 16777216 | tf_op jit(solution)/shard_map/reshape | solution.py:58
  656.3 13.2 %copy.19 = bf16[64,256,2,128]{3,2,1,0:T(2,128)(2,1)} copy(bf16[64,256,2,128]{3,0,2,1:T(8,128)(2,1)} %fusion.22) | data formatting | bytes 16777216 | tf_op jit(solution)/shard_map/transpose | solution.py:58
  669.4 14.1 %reshape.39 = bf16[64,256,256]{2,1,0:T(8,128)(2,1)} reshape(bf16[64,256,2,128]{3,2,1,0:T(2,128)(2,1)} %copy.19) | data formatting | bytes 16777216 | tf_op jit(solution)/shard_map/reshape | solution.py:58
  683.5 9.1 %gather_fusion = bf16[256,128,2,64]{1,3,2,0:T(8,128)(2,1)} fusion(bf16[1024,128,2,64]{1,3,2,0:T(8,128)(2,1)} %constant_dynamic-update-slice_fusion, s32[1024]{0:T(1024)S(1)} %get-tuple-element.23), kind=kCustom, calls=%fused_computation.clone | custom fusion | bytes 16778240 | tf_op jit(solution)/shard_map/jit(_take)/gather | solution.py:69
  700.2 12.9 %copy.18 = bf16[64,256,2,128]{1,3,2,0:T(8,128)(2,1)} copy(bf16[64,256,2,128]{3,0,2,1:T(8,128)(2,1)} %select_bitcast_fusion) | data formatting | bytes 16777216 | tf_op jit(solution)/shard_map/transpose | solution.py:58
  713.1 15.2 %fusion = bf16[1,64,256,512]{3,2,1,0:T(8,128)(2,1)} fusion(bf16[64,256,256]{1,2,0:T(8,128)(2,1)} %bitcast.27, bf16[64,256,256]{2,1,0:T(8,128)(2,1)} %reshape.40, bf16[64,256,256]{2,1,0:T(8,128)(2,1)} %reshape.39), kind=kOutput, calls=%fused_computation.3 | convolution fusion | flops 4345298944 | bytes 41943040 | tf_op jit(solution)/shard_map/fps,fqs->fpq/dot_general | solution.py:73
  (20 shorter events, 38.0 us)
Async XLA Ops:
  0.0 489.7 %copy-start = (s32[4,2]{0,1:T(2,128)S(1)}, s32[4,2]{0,1:T(2,128)}, u32[]{:S(2)}) copy-start(s32[4,2]{0,1:T(2,128)} %param.9) | copy-start | bytes 100
  298.4 193.3 %copy-start.2 = (s32[1024]{0:T(1024)S(1)}, s32[1024]{0:T(1024)}, u32[]{:S(2)}) copy-start(s32[1024]{0:T(1024)} %param.8) | copy-start | bytes 12292
  308.2 181.2 %collective-permute-start = (bf16[256,128,2,64]{1,3,2,0:T(8,128)(2,1)}, bf16[256,128,2,64]{1,3,2,0:T(8,128)(2,1)}, u32[]{:S(2)}, u32[]{:S(2)}) collective-permute-start(bf16[256,128,2,64]{1,3,2,0:T(8,128)(2,1)} %bitcast.22), channel_id=1, source_target_pairs={{0,1},{1,2},{2,3},{3,0},{4,5},{5,6},{6,7},{7,4},{8,9},{9,10},{10,1... | collective-permute-start | bytes 25165832 | tf_op jit(solution)/shard_map/ppermute | solution.py:28
  308.2 216.0 %collective-permute-start.1 = (bf16[256,128,2,64]{1,3,2,0:T(8,128)(2,1)}, bf16[256,128,2,64]{1,3,2,0:T(8,128)(2,1)}, u32[]{:S(2)}, u32[]{:S(2)}) collective-permute-start(bf16[256,128,2,64]{1,3,2,0:T(8,128)(2,1)} %bitcast.23), channel_id=1, source_target_pairs={{0,3},{1,0},{2,1},{3,2},{4,7},{5,4},{6,5},{7,6},{8,11},{9,8},{10,9... | collective-permute-start | bytes 25165832 | tf_op jit(solution)/shard_map/ppermute | solution.py:36
  489.4 93.2 %collective-permute-start.2 = (bf16[256,128,2,64]{1,3,2,0:T(8,128)(2,1)}, bf16[256,128,2,64]{1,3,2,0:T(8,128)(2,1)}, u32[]{:S(2)}, u32[]{:S(2)}) collective-permute-start(bf16[256,128,2,64]{1,3,2,0:T(8,128)(2,1)} %collective-permute-done), channel_id=1, source_target_pairs={{0,1},{1,2},{2,3},{3,0},{4,5},{5,6},{6,7},{7,4},{8,9},{9,10},{10,1... | collective-permute-start | bytes 25165832 | tf_op jit(solution)/shard_map/ppermute | solution.py:28
  713.1 15.2 %copy-start.1 = (s32[4,2]{0,1:T(2,128)S(1)}, s32[4,2]{0,1:T(2,128)}, u32[]{:S(2)}) copy-start(s32[4,2]{0,1:T(2,128)} %param.9) | copy-start | bytes 100
